TPU v7x, 128 devices: a whole 4x4x4 slice. The times are simulated.
128 devices in a mesh: segment: 8 (over x, core), dp: 16 (over z, y).
Axes of the slice: x: 4, y: 4, z: 4, core: 2. Of those that a mesh axis runs over, the one named last changes fastest.
Arguments:
- embeds: bfloat16 [2, 16, 128, 4096], P(None, 'dp'), may hold values from -6 to 6
- base_weight: bfloat16 [8, 4096, 4096], P('segment', 'dp'), may hold values from -0.09375 to 0.09375
- norm_gain: float32 [8, 4096], P('segment'), may hold values from 0.25 to 1.75
- skill_down: bfloat16 [8, 16, 8, 4096], P('segment'), may hold values from -0.09375 to 0.09375
- skill_up: bfloat16 [8, 16, 8, 4096], P('segment'), may hold values from -2 to 2
- task_ids: int32 [2, 16], replicated, may hold values from 0 to 1835
- allocation: int32 [1836, 16], replicated, may hold values 0 or 1
- target_lengths: int32 [2, 16], replicated, may hold values from 1 to 128
- cotangent: bfloat16 [2, 16, 128, 4096], P(None, 'dp'), may hold values from -6 to 6
Outputs:
- hidden: bfloat16 [8, 2, 16, 128, 4096], P('segment', None, 'dp')
- input_grads: bfloat16 [8, 2, 16, 128, 4096], P('segment', None, 'dp')
- grad_down: float32 [8, 16, 8, 4096], P('segment', None, None, 'dp')
- grad_up: float32 [8, 16, 8, 4096], P('segment', None, None, 'dp')
All inputs are finite; a program needn't handle non-finite values.
Results may differ from a plain program's by a relative error of at most 0.019.
Values may be sent and summed in bfloat16 or wider, within the bound.
A program may use at most 192 MiB of HBM per device.

v0:
```python
import jax
import jax.numpy as jnp
from jax import lax
from jax.sharding import PartitionSpec as P

EPS = 1e-06


def shifted(block, axis, distance):
    devices = range(lax.axis_size(axis))
    route = [(i - distance, i) for i in devices if i - distance in devices]
    return lax.ppermute(block, axis, route)


def in_blocks(x, dim, size):
    before, after = (x.shape[:dim], x.shape[dim + 1 :])
    return jnp.moveaxis(x.reshape(*before, size, -1, *after), dim, 0)


def sent_and_summed(x, axis, dim):
    size = lax.axis_size(axis)
    parts = lax.all_to_all(in_blocks(x, dim, size), axis, 0, 0, tiled=True)
    return jnp.sum(parts.astype(jnp.float32), axis=0)


def side_by_side(arrays, axis, dim, along):
    both = jnp.concatenate(arrays, axis=along)
    result, at, done = (sent_and_summed(both, axis, dim), 0, [])
    for a in arrays:
        done.append(lax.slice_in_dim(result, at, at + a.shape[along], axis=along))
        at += a.shape[along]
    return tuple(done)


def prepare(x, gain, down_t):
    xf = x.astype(jnp.float32)
    inv = lax.rsqrt(jnp.mean(xf * xf, axis=-1, keepdims=True) + EPS)
    normed = (xf * inv * gain).astype(jnp.bfloat16)
    low = jnp.dot(normed, down_t.T, preferred_element_type=jnp.float32).astype(jnp.bfloat16)
    return (normed, low, inv)


def forward_full(x, weight, gain, down_t, up_t):
    normed, low, inv = prepare(x, gain, down_t)
    total = x.astype(jnp.float32) + jnp.dot(normed, weight, preferred_element_type=jnp.float32)
    total = total + jnp.dot(low, up_t, preferred_element_type=jnp.float32)
    return (total.astype(jnp.bfloat16), normed, low, inv)


def backward_core(x, normed, low, inv, grad_out, weight, gain, down_t, up_t):
    g_low = jnp.dot(grad_out, up_t.T, preferred_element_type=jnp.float32).astype(jnp.bfloat16)
    dnorm = jnp.dot(grad_out, weight.T, preferred_element_type=jnp.float32)
    dnorm = dnorm + jnp.dot(g_low, down_t, preferred_element_type=jnp.float32)
    seq_down = jnp.dot(g_low.T, normed, preferred_element_type=jnp.float32)
    seq_up = jnp.dot(low.T, grad_out, preferred_element_type=jnp.float32)
    xf = x.astype(jnp.float32)
    scaled = gain * dnorm
    grad_in = (
        grad_out.astype(jnp.float32)
        + inv * scaled
        - xf * inv * inv * inv * jnp.mean(xf * scaled, axis=-1, keepdims=True)
    )
    return (grad_in.astype(jnp.bfloat16), seq_down, seq_up)


def pick(table, index):
    return lax.dynamic_index_in_dim(table, index, 0, keepdims=False)


def place(table, value, index, active):
    return jnp.where(active, lax.dynamic_update_index_in_dim(table, value, index, 0), table)


def shards(
    embeds,
    base_weight,
    norm_gain,
    skill_down,
    skill_up,
    task_ids,
    allocation,
    target_lengths,
    cotangent,
):
    segments = lax.axis_size("segment")
    segment = lax.axis_index("segment")
    member = lax.axis_index("dp")
    weight = lax.all_gather(base_weight[0], "dp", axis=0, tiled=True)
    gain = norm_gain[0]
    micro = embeds.shape[0]
    rows = embeds.shape[2]
    width = embeds.shape[3]
    splits = 1
    blocks = micro * splits
    block_rows = rows // splits
    tasks = lax.dynamic_index_in_dim(task_ids, member, 1, keepdims=False)
    lengths = lax.dynamic_index_in_dim(target_lengths, member, 1, keepdims=False)
    onehot = (tasks[:, None] == jnp.arange(allocation.shape[0], dtype=jnp.int32)[None, :]).astype(
        jnp.float32
    )
    alloc = allocation.astype(jnp.float32)
    counts = jnp.maximum(jnp.sum(alloc, axis=1, keepdims=True), 1.0)
    mix = jnp.einsum("mt,ts->ms", onehot, alloc / counts, precision=lax.Precision.HIGHEST)
    down_seq = jnp.einsum(
        "ms,srd->mrd", mix, skill_down[0].astype(jnp.float32), precision=lax.Precision.HIGHEST
    ).astype(jnp.bfloat16)
    up_seq = jnp.einsum(
        "ms,srd->mrd", mix, skill_up[0].astype(jnp.float32), precision=lax.Precision.HIGHEST
    ).astype(jnp.bfloat16)
    down_all = jnp.repeat(down_seq, splits, axis=0)
    up_all = jnp.repeat(up_seq, splits, axis=0)
    mix_all = jnp.repeat(mix, splits, axis=0)
    firsts = embeds[:, 0]
    live = jnp.arange(rows, dtype=jnp.int32)[None, :] < lengths[:, None]
    seeds = cotangent[:, 0] * live[..., None].astype(jnp.bfloat16)
    ticks = segments + blocks - 1
    rank = down_all.shape[1]
    blank = jnp.zeros((block_rows, width), jnp.bfloat16)
    stack_blank = jnp.zeros((blocks, block_rows, width), jnp.bfloat16)
    low_blank = jnp.zeros((blocks, block_rows, rank), jnp.bfloat16)
    inv_blank = jnp.zeros((blocks, block_rows, 1), jnp.float32)

    def forward_tick(tick, carry):
        incoming, saved, outs, kept_norm, kept_low, kept_inv = carry
        slot = tick - segment
        active = (slot >= 0) & (slot < blocks)
        index = jnp.clip(slot, 0, blocks - 1)
        x = jnp.where(segment == 0, pick(firsts, index), incoming)
        result, normed, low, inv = lax.cond(
            active,
            lambda: forward_full(x, weight, gain, pick(down_all, index), pick(up_all, index)),
            lambda: (
                blank,
                blank,
                jnp.zeros((block_rows, rank), jnp.bfloat16),
                jnp.zeros((block_rows, 1), jnp.float32),
            ),
        )
        saved = place(saved, x, index, active)
        outs = place(outs, result, index, active)
        return (result, (saved, outs, kept_norm, kept_low, kept_inv))

    def forward_step(tick, carry):
        result, rest = forward_tick(tick, carry)
        moved = shifted(result, "segment", 1)
        return (moved,) + rest

    carry = (blank, stack_blank, stack_blank, stack_blank, low_blank, inv_blank)
    carry = lax.fori_loop(0, ticks - 1, forward_step, carry)
    _, (saved, outs, kept_norm, kept_low, kept_inv) = forward_tick(ticks - 1, carry)
    skills = skill_down.shape[1]
    acc_blank = jnp.zeros((skills, rank, width), jnp.float32)

    def backward_tick(tick, carry):
        incoming, grads_in, acc_down, acc_up = carry
        slot = tick - (segments - 1 - segment)
        active = (slot >= 0) & (slot < blocks)
        index = jnp.clip(slot, 0, blocks - 1)
        grad_out = jnp.where(segment == segments - 1, pick(seeds, index), incoming)
        x = pick(saved, index)
        down_t = pick(down_all, index)
        up_t = pick(up_all, index)

        def run():
            normed, low, inv = prepare(x, gain, down_t)
            return backward_core(x, normed, low, inv, grad_out, weight, gain, down_t, up_t)

        grad_in, seq_down, seq_up = lax.cond(
            active,
            run,
            lambda: (
                blank,
                jnp.zeros((rank, width), jnp.float32),
                jnp.zeros((rank, width), jnp.float32),
            ),
        )
        weights = pick(mix_all, index)[:, None, None]
        acc_down = acc_down + weights * seq_down[None]
        acc_up = acc_up + weights * seq_up[None]
        grads_in = place(grads_in, grad_in, index, active)
        return (grad_in, (grads_in, acc_down, acc_up))

    def backward_step(tick, carry):
        grad_in, rest = backward_tick(tick, carry)
        moved = shifted(grad_in, "segment", -1)
        return (moved,) + rest

    carry = (blank, stack_blank, acc_blank, acc_blank)
    carry = lax.fori_loop(0, ticks - 1, backward_step, carry)
    _, (grads_in, acc_down, acc_up) = backward_tick(ticks - 1, carry)
    grad_down, grad_up = side_by_side(
        (acc_down.astype(jnp.bfloat16), acc_up.astype(jnp.bfloat16)), "dp", 2, 0
    )
    return (outs[None, :, None], grads_in[None, :, None], grad_down[None], grad_up[None])


def solution(mesh):
    in_specs = (
        P(None, "dp", None, None),
        P("segment", "dp", None),
        P("segment", None),
        P("segment", None, None, None),
        P("segment", None, None, None),
        P(),
        P(),
        P(),
        P(None, "dp", None, None),
    )
    out_specs = (
        P("segment", None, "dp", None, None),
        P("segment", None, "dp", None, None),
        P("segment", None, None, "dp"),
        P("segment", None, None, "dp"),
    )
    return jax.shard_map(shards, mesh=mesh, in_specs=in_specs, out_specs=out_specs, check_vma=False)
```

profile of v0, /device:TPU:0, one launch (start us, length us, event | category | flops | bytes accessed | tf_op | source)
XLA Modules:
  0.0 870.6 jit_solution(13723919812734326416)
XLA Ops:
  13.2 3.1 bitcast_multiply_fusion
  16.4 193.5 %all-gather.3.cloned.1.call-done = bf16[1,4096,4096]{2,1,0:T(8,128)(2,1)} async-done(((bf16[1,256,4096]{2,1,0:T(8,128)(2,1)}), bf16[1,4096,4096]{2,1,0:T(8,128)(2,1)}) %all-gather.3.cloned.1.call-update) | async-done | bytes 33554448 | tf_op jit(solution)/shard_map/all_gather | solution.py:88
  212.8 230.3 %while.40 = (s32[]{:T(128)}, bf16[128,4096]{1,0:T(8,128)(2,1)}, bf16[2,128,4096]{2,1,0:T(8,128)(2,1)S(1)}, bf16[2,128,4096]{2,1,0:T(8,128)(2,1)}, s32[]{:T(128)}...) while((s32[]{:T(128)}, bf16[128,4096]{1,0:T(8,128)(2,1)}, ...), condition=%wide.region_5.6_spmd, body=%wide.region_1.5_spmd.sunk | while | flops 4321182720 | bytes 60985708 | solution.py:149
  214.7 23.2 %conditional.9 = (bf16[128,4096]{1,0:T(8,128)(2,1)}, bf16[1,128,4096]{2,1,0:T(8,128)(2,1)}) conditional(s32[]{:T(128)} %convert_element_type.345, () %tuple.153, (bf16[128,4096]{1,0:T(8,128)(2,1)S(1)}, f32[1,4096]{1,0:T(1,128)S(1)}, bf16[4096,4096]{1,0:T(8,128)(2,1)}, s32[]{:T(128)}, bf16[2,8,4096]{2,1,0:T(8,128)(2,1)S(1)}, ...), branch_computations={%region_2.2_spmd, %region_3.4_spmd} | conditional | flops 4319609856 | bytes 44207664 | solution.py:129
  215.0 16.5 %convolution_add_fusion.1 = f32[128,4096]{1,0:T(8,128)} fusion(bf16[4096,4096]{1,0:T(8,128)(2,1)} %get-tuple-element.684, bf16[128,4096]{1,0:T(8,128)(2,1)S(1)} %get-tuple-element.682, f32[4096]{0:T(1024)S(1)} %bitcast.186, f32[128]{0:T(128)S(1)} %add_rsqrt_fusion), kind=kOutput, calls=%fused_computation.1 | convolution fusion | flops 4298113024 | bytes 36717056 | tf_op jit(solution)/shard_map/while/body/eval_jaxpr/cond/branch_1_fun/dot_general | solution.py:45
  231.5 4.1 fusion
  239.2 2.8 select_dynamic-update-slice_fusion.4
  244.8 23.2 %conditional.9 = (bf16[128,4096]{1,0:T(8,128)(2,1)}, bf16[1,128,4096]{2,1,0:T(8,128)(2,1)}) conditional(s32[]{:T(128)} %convert_element_type.345, () %tuple.153, (bf16[128,4096]{1,0:T(8,128)(2,1)S(1)}, f32[1,4096]{1,0:T(1,128)S(1)}, bf16[4096,4096]{1,0:T(8,128)(2,1)}, s32[]{:T(128)}, bf16[2,8,4096]{2,1,0:T(8,128)(2,1)S(1)}, ...), branch_computations={%region_2.2_spmd, %region_3.4_spmd} | conditional | flops 4319609856 | bytes 44207664 | solution.py:129
  245.1 16.5 %convolution_add_fusion.1 = f32[128,4096]{1,0:T(8,128)} fusion(bf16[4096,4096]{1,0:T(8,128)(2,1)} %get-tuple-element.684, bf16[128,4096]{1,0:T(8,128)(2,1)S(1)} %get-tuple-element.682, f32[4096]{0:T(1024)S(1)} %bitcast.186, f32[128]{0:T(128)S(1)} %add_rsqrt_fusion), kind=kOutput, calls=%fused_computation.1 | convolution fusion | flops 4298113024 | bytes 36717056 | tf_op jit(solution)/shard_map/while/body/eval_jaxpr/cond/branch_1_fun/dot_general | solution.py:45
  261.6 4.1 fusion
  270.2 2.8 select_dynamic-update-slice_fusion.4
  278.1 32.4 %collective-permute-start = (bf16[128,4096]{1,0:T(8,128)(2,1)}, bf16[128,4096]{1,0:T(8,128)(2,1)S(1)}, u32[]{:S(2)}, u32[]{:S(2)}) collective-permute-start(bf16[128,4096]{1,0:T(8,128)(2,1)} %get-tuple-element.1159), channel_id=1, source_target_pairs={{0,16},{16,32},{32,48},{48,64},{64,80},{80,96},{96,112},{1,17},{17... | collective-permute-start | bytes 3145736 | tf_op jit(solution)/shard_map/while/body/eval_jaxpr/ppermute | solution.py:12
  318.0 14.1 %collective-permute-start = (bf16[128,4096]{1,0:T(8,128)(2,1)}, bf16[128,4096]{1,0:T(8,128)(2,1)S(1)}, u32[]{:S(2)}, u32[]{:S(2)}) collective-permute-start(bf16[128,4096]{1,0:T(8,128)(2,1)} %get-tuple-element.1159), channel_id=1, source_target_pairs={{0,16},{16,32},{32,48},{48,64},{64,80},{80,96},{96,112},{1,17},{17... | collective-permute-start | bytes 3145736 | tf_op jit(solution)/shard_map/while/body/eval_jaxpr/ppermute | solution.py:12
  332.1 2.5 select_dynamic-update-slice_fusion.4
  339.6 35.1 %collective-permute-start = (bf16[128,4096]{1,0:T(8,128)(2,1)}, bf16[128,4096]{1,0:T(8,128)(2,1)S(1)}, u32[]{:S(2)}, u32[]{:S(2)}) collective-permute-start(bf16[128,4096]{1,0:T(8,128)(2,1)} %get-tuple-element.1159), channel_id=1, source_target_pairs={{0,16},{16,32},{32,48},{48,64},{64,80},{80,96},{96,112},{1,17},{17... | collective-permute-start | bytes 3145736 | tf_op jit(solution)/shard_map/while/body/eval_jaxpr/ppermute | solution.py:12
  374.7 2.5 select_dynamic-update-slice_fusion.4
  382.3 14.1 %collective-permute-start = (bf16[128,4096]{1,0:T(8,128)(2,1)}, bf16[128,4096]{1,0:T(8,128)(2,1)S(1)}, u32[]{:S(2)}, u32[]{:S(2)}) collective-permute-start(bf16[128,4096]{1,0:T(8,128)(2,1)} %get-tuple-element.1159), channel_id=1, source_target_pairs={{0,16},{16,32},{32,48},{48,64},{64,80},{80,96},{96,112},{1,17},{17... | collective-permute-start | bytes 3145736 | tf_op jit(solution)/shard_map/while/body/eval_jaxpr/ppermute | solution.py:12
  403.9 14.1 %collective-permute-start = (bf16[128,4096]{1,0:T(8,128)(2,1)}, bf16[128,4096]{1,0:T(8,128)(2,1)S(1)}, u32[]{:S(2)}, u32[]{:S(2)}) collective-permute-start(bf16[128,4096]{1,0:T(8,128)(2,1)} %get-tuple-element.1159), channel_id=1, source_target_pairs={{0,16},{16,32},{32,48},{48,64},{64,80},{80,96},{96,112},{1,17},{17... | collective-permute-start | bytes 3145736 | tf_op jit(solution)/shard_map/while/body/eval_jaxpr/ppermute | solution.py:12
  418.0 2.5 select_dynamic-update-slice_fusion.4
  425.5 14.1 %collective-permute-start = (bf16[128,4096]{1,0:T(8,128)(2,1)}, bf16[128,4096]{1,0:T(8,128)(2,1)S(1)}, u32[]{:S(2)}, u32[]{:S(2)}) collective-permute-start(bf16[128,4096]{1,0:T(8,128)(2,1)} %get-tuple-element.1159), channel_id=1, source_target_pairs={{0,16},{16,32},{32,48},{48,64},{64,80},{80,96},{96,112},{1,17},{17... | collective-permute-start | bytes 3145736 | tf_op jit(solution)/shard_map/while/body/eval_jaxpr/ppermute | solution.py:12
  439.6 2.5 select_dynamic-update-slice_fusion.4
  443.1 2.8 fusion.140
  448.6 355.2 %while.41 = (s32[]{:T(128)}, bf16[128,4096]{1,0:T(8,128)(2,1)}, bf16[2,128,4096]{2,1,0:T(8,128)(2,1)}, f32[16,8,4096]{2,1,0:T(8,128)}, f32[16,8,4096]{2,1,0:T(8,...) while((s32[]{:T(128)}, bf16[128,4096]{1,0:T(8,128)(2,1)}, ...), condition=%wide.region_14.15_spmd.clone, body=%wide.region_9.14_spmd.clone.sunk | while | flops 4354214400 | bytes 94118616 | solution.py:189
  455.5 2.7 select_add_fusion.3
  458.2 25.3 %collective-permute-done.1 = bf16[128,4096]{1,0:T(8,128)(2,1)S(1)} collective-permute-done((bf16[128,4096]{1,0:T(8,128)(2,1)}, bf16[128,4096]{1,0:T(8,128)(2,1)S(1)}, u32[]{:S(2)}, u32[]{:S(2)}) %collective-permute-start.1) | collective-permute-done | bytes 1048608 | tf_op jit(solution)/shard_map/while/body/eval_jaxpr/ppermute | solution.py:12
  491.3 4.3 select_add_fusion.3
  495.6 8.0 collective-permute-done.1
  511.6 4.3 select_add_fusion.3
  515.9 7.4 collective-permute-done.1
  531.2 4.3 select_add_fusion.3
  535.5 7.9 collective-permute-done.1
  551.2 4.3 select_add_fusion.3
  555.5 23.4 %collective-permute-done.1 = bf16[128,4096]{1,0:T(8,128)(2,1)S(1)} collective-permute-done((bf16[128,4096]{1,0:T(8,128)(2,1)}, bf16[128,4096]{1,0:T(8,128)(2,1)S(1)}, u32[]{:S(2)}, u32[]{:S(2)}) %collective-permute-start.1) | collective-permute-done | bytes 1048608 | tf_op jit(solution)/shard_map/while/body/eval_jaxpr/ppermute | solution.py:12
  586.8 4.3 select_add_fusion.3
  591.1 8.0 collective-permute-done.1
  607.0 4.3 select_add_fusion.3
  611.3 148.2 %collective-permute-done.1 = bf16[128,4096]{1,0:T(8,128)(2,1)S(1)} collective-permute-done((bf16[128,4096]{1,0:T(8,128)(2,1)}, bf16[128,4096]{1,0:T(8,128)(2,1)S(1)}, u32[]{:S(2)}, u32[]{:S(2)}) %collective-permute-start.1) | collective-permute-done | bytes 1048608 | tf_op jit(solution)/shard_map/while/body/eval_jaxpr/ppermute | solution.py:12
  760.5 25.9 %conditional.10 = (bf16[128,4096]{1,0:T(8,128)(2,1)}, f32[8,4096]{1,0:T(8,128)S(1)}, f32[8,4096]{1,0:T(8,128)S(1)}, bf16[1,128,4096]{2,1,0:T(8,128)(2,1)}) conditional(s32[]{:T(128)} %convert_element_type.346, () %tuple.157, (pred[]{:T(512)}, bf16[2,128,4096]{2,1,0:T(8,128)(2,1)}, s32[]{:T(128)}, bf16[128,4096]{1,0:T(8,128)(2,1)}, ...), branch_computations={%region_10.10_spmd, %region_11.13_spmd} | conditional | flops 4350544384 | bytes 57155172 | solution.py:168
  763.4 16.0 %fusion.153 = f32[128,4096]{1,0:T(8,128)S(1)} fusion(bf16[128,4096]{1,0:T(8,128)(2,1)S(1)} %bitcast_select_fusion.2, bf16[4096,4096]{1,0:T(8,128)(2,1)} %get-tuple-element.714), kind=kOutput, calls=%fused_computation.169 | convolution fusion | flops 4294967296 | bytes 36700160 | tf_op jit(solution)/shard_map/while/body/eval_jaxpr/cond/branch_1_fun/dot_general | solution.py:52
  788.6 2.8 select_dynamic-update-slice_fusion.5
  791.4 4.3 select_add_fusion.3
  795.7 7.1 collective-permute-done.1
  803.8 23.6 %conditional.5 = (f32[8,4096]{1,0:T(8,128)}, f32[8,4096]{1,0:T(8,128)}, bf16[1,128,4096]{2,1,0:T(8,128)(2,1)}) conditional(s32[]{:T(128)} %convert_element_type.171, () %tuple.98, (pred[]{:T(512)}, bf16[2,128,4096]{2,1,0:T(8,128)(2,1)}, s32[]{:T(128)}, bf16[128,4096]{1,0:T(8,128)(2,1)}, bf16[2,8,4096]{2,0,1:T(2,128)(2,1)}, ...), branch_computations={%region_15.16_spmd, %region_16.19_spmd} | conditional | flops 4350544384 | bytes 56620128 | solution.py:168
  805.9 16.0 %fusion.154 = f32[128,4096]{1,0:T(8,128)S(1)} fusion(bf16[128,4096]{1,0:T(8,128)(2,1)S(1)} %bitcast_select_fusion.3, bf16[4096,4096]{1,0:T(8,128)(2,1)} %get-tuple-element.744), kind=kOutput, calls=%fused_computation.170 | convolution fusion | flops 4294967296 | bytes 36700160 | tf_op jit(solution)/shard_map/cond/branch_1_fun/dot_general | solution.py:52
  827.3 2.8 add_convert_fusion.1
  833.1 5.5 all-to-all-start
  843.7 4.0 bitcast_dynamic-update-slice_fusion
  847.8 13.3 %all-to-all-done = bf16[16,32,8,256]{3,2,1,0:T(8,128)(2,1)} async-done(((bf16[16,32,8,256]{3,2,1,0:T(8,128)(2,1)}), bf16[16,32,8,256]{3,2,1,0:T(8,128)(2,1)}, u32[]{:S(2)}, u32[]{:S(2)}) %all-to-all-start) | async-done | bytes 2097184 | tf_op jit(solution)/shard_map/all_to_all | solution.py:22
  (250 shorter events, 176.8 us)
Async XLA Ops:
  7.2 2.9 copy-start.16
  7.2 202.7 %all-gather.3.cloned.1.call-start = ((), (), s32[]{:S(2)}) async-start(), calls=%async_computation.1 | async-start | bytes 35651584 | tf_op jit(solution)/shard_map/all_gather | solution.py:88
  7.9 4.5 copy-start.23
  8.5 7.9 copy-start.21
  10.1 6.3 copy-start.10
  11.7 4.6 copy-start.13
  210.1 2.7 copy-start.9
  237.8 4.1 collective-permute-start
  268.0 5.1 collective-permute-start
  278.1 34.9 %collective-permute-start = (bf16[128,4096]{1,0:T(8,128)(2,1)}, bf16[128,4096]{1,0:T(8,128)(2,1)S(1)}, u32[]{:S(2)}, u32[]{:S(2)}) collective-permute-start(bf16[128,4096]{1,0:T(8,128)(2,1)} %get-tuple-element.1159), channel_id=1, source_target_pairs={{0,16},{16,32},{32,48},{48,64},{64,80},{80,96},{96,112},{1,17},{17... | collective-permute-start | bytes 3145736 | tf_op jit(solution)/shard_map/while/body/eval_jaxpr/ppermute | solution.py:12
  318.0 16.6 %collective-permute-start = (bf16[128,4096]{1,0:T(8,128)(2,1)}, bf16[128,4096]{1,0:T(8,128)(2,1)S(1)}, u32[]{:S(2)}, u32[]{:S(2)}) collective-permute-start(bf16[128,4096]{1,0:T(8,128)(2,1)} %get-tuple-element.1159), channel_id=1, source_target_pairs={{0,16},{16,32},{32,48},{48,64},{64,80},{80,96},{96,112},{1,17},{17... | collective-permute-start | bytes 3145736 | tf_op jit(solution)/shard_map/while/body/eval_jaxpr/ppermute | solution.py:12
  339.6 37.6 %collective-permute-start = (bf16[128,4096]{1,0:T(8,128)(2,1)}, bf16[128,4096]{1,0:T(8,128)(2,1)S(1)}, u32[]{:S(2)}, u32[]{:S(2)}) collective-permute-start(bf16[128,4096]{1,0:T(8,128)(2,1)} %get-tuple-element.1159), channel_id=1, source_target_pairs={{0,16},{16,32},{32,48},{48,64},{64,80},{80,96},{96,112},{1,17},{17... | collective-permute-start | bytes 3145736 | tf_op jit(solution)/shard_map/while/body/eval_jaxpr/ppermute | solution.py:12
  382.3 16.6 %collective-permute-start = (bf16[128,4096]{1,0:T(8,128)(2,1)}, bf16[128,4096]{1,0:T(8,128)(2,1)S(1)}, u32[]{:S(2)}, u32[]{:S(2)}) collective-permute-start(bf16[128,4096]{1,0:T(8,128)(2,1)} %get-tuple-element.1159), channel_id=1, source_target_pairs={{0,16},{16,32},{32,48},{48,64},{64,80},{80,96},{96,112},{1,17},{17... | collective-permute-start | bytes 3145736 | tf_op jit(solution)/shard_map/while/body/eval_jaxpr/ppermute | solution.py:12
  403.9 16.6 %collective-permute-start = (bf16[128,4096]{1,0:T(8,128)(2,1)}, bf16[128,4096]{1,0:T(8,128)(2,1)S(1)}, u32[]{:S(2)}, u32[]{:S(2)}) collective-permute-start(bf16[128,4096]{1,0:T(8,128)(2,1)} %get-tuple-element.1159), channel_id=1, source_target_pairs={{0,16},{16,32},{32,48},{48,64},{64,80},{80,96},{96,112},{1,17},{17... | collective-permute-start | bytes 3145736 | tf_op jit(solution)/shard_map/while/body/eval_jaxpr/ppermute | solution.py:12
  425.5 16.6 %collective-permute-start = (bf16[128,4096]{1,0:T(8,128)(2,1)}, bf16[128,4096]{1,0:T(8,128)(2,1)S(1)}, u32[]{:S(2)}, u32[]{:S(2)}) collective-permute-start(bf16[128,4096]{1,0:T(8,128)(2,1)} %get-tuple-element.1159), channel_id=1, source_target_pairs={{0,16},{16,32},{32,48},{48,64},{64,80},{80,96},{96,112},{1,17},{17... | collective-permute-start | bytes 3145736 | tf_op jit(solution)/shard_map/while/body/eval_jaxpr/ppermute | solution.py:12
  450.8 32.6 %collective-permute-start.1 = (bf16[128,4096]{1,0:T(8,128)(2,1)}, bf16[128,4096]{1,0:T(8,128)(2,1)S(1)}, u32[]{:S(2)}, u32[]{:S(2)}) collective-permute-start(bf16[128,4096]{1,0:T(8,128)(2,1)} %get-tuple-element.1176), channel_id=1, source_target_pairs={{16,0},{32,16},{48,32},{64,48},{80,64},{96,80},{112,96},{17,1},{33... | collective-permute-start | bytes 3145736 | tf_op jit(solution)/shard_map/while/body/eval_jaxpr/ppermute | solution.py:12
  452.1 3.3 copy-start.2
  458.2 25.3 %copy-start.3 = (f32[16,8,4096]{2,1,0:T(8,128)}, f32[16,8,4096]{2,1,0:T(8,128)S(1)}, u32[]{:S(2)}) copy-start(f32[16,8,4096]{2,1,0:T(8,128)S(1)} %get-tuple-element.1273) | copy-start | bytes 6291460 | tf_op jit(solution)/shard_map/while
  486.7 17.0 %collective-permute-start.1 = (bf16[128,4096]{1,0:T(8,128)(2,1)}, bf16[128,4096]{1,0:T(8,128)(2,1)S(1)}, u32[]{:S(2)}, u32[]{:S(2)}) collective-permute-start(bf16[128,4096]{1,0:T(8,128)(2,1)} %get-tuple-element.1176), channel_id=1, source_target_pairs={{16,0},{32,16},{48,32},{64,48},{80,64},{96,80},{112,96},{17,1},{33... | collective-permute-start | bytes 3145736 | tf_op jit(solution)/shard_map/while/body/eval_jaxpr/ppermute | solution.py:12
  488.0 3.3 copy-start.2
  495.6 8.1 copy-start.3
  506.9 16.3 %collective-permute-start.1 = (bf16[128,4096]{1,0:T(8,128)(2,1)}, bf16[128,4096]{1,0:T(8,128)(2,1)S(1)}, u32[]{:S(2)}, u32[]{:S(2)}) collective-permute-start(bf16[128,4096]{1,0:T(8,128)(2,1)} %get-tuple-element.1176), channel_id=1, source_target_pairs={{16,0},{32,16},{48,32},{64,48},{80,64},{96,80},{112,96},{17,1},{33... | collective-permute-start | bytes 3145736 | tf_op jit(solution)/shard_map/while/body/eval_jaxpr/ppermute | solution.py:12
  508.2 3.3 copy-start.2
  515.9 7.4 copy-start.3
  526.5 16.8 %collective-permute-start.1 = (bf16[128,4096]{1,0:T(8,128)(2,1)}, bf16[128,4096]{1,0:T(8,128)(2,1)S(1)}, u32[]{:S(2)}, u32[]{:S(2)}) collective-permute-start(bf16[128,4096]{1,0:T(8,128)(2,1)} %get-tuple-element.1176), channel_id=1, source_target_pairs={{16,0},{32,16},{48,32},{64,48},{80,64},{96,80},{112,96},{17,1},{33... | collective-permute-start | bytes 3145736 | tf_op jit(solution)/shard_map/while/body/eval_jaxpr/ppermute | solution.py:12
  527.8 3.3 copy-start.2
  535.4 7.9 copy-start.3
  546.6 32.3 %collective-permute-start.1 = (bf16[128,4096]{1,0:T(8,128)(2,1)}, bf16[128,4096]{1,0:T(8,128)(2,1)S(1)}, u32[]{:S(2)}, u32[]{:S(2)}) collective-permute-start(bf16[128,4096]{1,0:T(8,128)(2,1)} %get-tuple-element.1176), channel_id=1, source_target_pairs={{16,0},{32,16},{48,32},{64,48},{80,64},{96,80},{112,96},{17,1},{33... | collective-permute-start | bytes 3145736 | tf_op jit(solution)/shard_map/while/body/eval_jaxpr/ppermute | solution.py:12
  547.9 3.3 copy-start.2
  555.5 23.4 %copy-start.3 = (f32[16,8,4096]{2,1,0:T(8,128)}, f32[16,8,4096]{2,1,0:T(8,128)S(1)}, u32[]{:S(2)}) copy-start(f32[16,8,4096]{2,1,0:T(8,128)S(1)} %get-tuple-element.1273) | copy-start | bytes 6291460 | tf_op jit(solution)/shard_map/while
  582.2 17.0 %collective-permute-start.1 = (bf16[128,4096]{1,0:T(8,128)(2,1)}, bf16[128,4096]{1,0:T(8,128)(2,1)S(1)}, u32[]{:S(2)}, u32[]{:S(2)}) collective-permute-start(bf16[128,4096]{1,0:T(8,128)(2,1)} %get-tuple-element.1176), channel_id=1, source_target_pairs={{16,0},{32,16},{48,32},{64,48},{80,64},{96,80},{112,96},{17,1},{33... | collective-permute-start | bytes 3145736 | tf_op jit(solution)/shard_map/while/body/eval_jaxpr/ppermute | solution.py:12
  583.5 3.3 copy-start.2
  591.1 8.1 copy-start.3
  602.4 157.1 %collective-permute-start.1 = (bf16[128,4096]{1,0:T(8,128)(2,1)}, bf16[128,4096]{1,0:T(8,128)(2,1)S(1)}, u32[]{:S(2)}, u32[]{:S(2)}) collective-permute-start(bf16[128,4096]{1,0:T(8,128)(2,1)} %get-tuple-element.1176), channel_id=1, source_target_pairs={{16,0},{32,16},{48,32},{64,48},{80,64},{96,80},{112,96},{17,1},{33... | collective-permute-start | bytes 3145736 | tf_op jit(solution)/shard_map/while/body/eval_jaxpr/ppermute | solution.py:12
  603.7 3.3 copy-start.2
  611.3 148.2 %copy-start.3 = (f32[16,8,4096]{2,1,0:T(8,128)}, f32[16,8,4096]{2,1,0:T(8,128)S(1)}, u32[]{:S(2)}) copy-start(f32[16,8,4096]{2,1,0:T(8,128)S(1)} %get-tuple-element.1273) | copy-start | bytes 6291460 | tf_op jit(solution)/shard_map/while
  763.4 16.0 %copy-start.17 = (bf16[128,8]{0,1:T(8,128)(2,1)}, bf16[128,8]{0,1:T(8,128)(2,1)S(1)}, u32[]{:S(2)}) copy-start(bf16[128,8]{0,1:T(8,128)(2,1)S(1)} %convolution_convert_fusion.1) | copy-start | bytes 6148 | tf_op jit(solution)/shard_map/while/body/eval_jaxpr/cond
  780.2 4.2 copy-start.19
  786.5 16.3 %collective-permute-start.1 = (bf16[128,4096]{1,0:T(8,128)(2,1)}, bf16[128,4096]{1,0:T(8,128)(2,1)S(1)}, u32[]{:S(2)}, u32[]{:S(2)}) collective-permute-start(bf16[128,4096]{1,0:T(8,128)(2,1)} %get-tuple-element.1176), channel_id=1, source_target_pairs={{16,0},{32,16},{48,32},{64,48},{80,64},{96,80},{112,96},{17,1},{33... | collective-permute-start | bytes 3145736 | tf_op jit(solution)/shard_map/while/body/eval_jaxpr/ppermute | solution.py:12
  787.7 3.6 copy-start.2
  795.7 7.1 copy-start.3
  805.9 16.0 %copy-start.12 = (bf16[2,8,4096]{2,0,1:T(2,128)(2,1)S(1)}, bf16[2,8,4096]{2,0,1:T(2,128)(2,1)}, u32[]{:S(2)}) copy-start(bf16[2,8,4096]{2,0,1:T(2,128)(2,1)} %get-tuple-element.936) | copy-start | bytes 393220 | tf_op jit(solution)/shard_map/cond
  833.1 5.5 copy-start.4
  833.1 28.0 %all-to-all-start = ((bf16[16,32,8,256]{3,2,1,0:T(8,128)(2,1)}), bf16[16,32,8,256]{3,2,1,0:T(8,128)(2,1)}, u32[]{:S(2)}, u32[]{:S(2)}) async-start(bf16[16,32,8,256]{3,2,1,0:T(8,128)(2,1)} %copy.43), calls=%async_computation | async-start | bytes 4194304 | tf_op jit(solution)/shard_map/all_to_all | solution.py:22
  838.7 2.6 copy-start.8
  838.7 2.6 copy-start.11
  838.7 2.6 copy-start.14
  843.7 20.0 %copy-start.1 = (bf16[1,16,8,4096]{3,2,1,0:T(8,128)(2,1)S(1)}, bf16[1,16,8,4096]{3,2,1,0:T(8,128)(2,1)}, u32[]{:S(2)}) copy-start(bf16[1,16,8,4096]{3,2,1,0:T(8,128)(2,1)} %param.24) | copy-start | bytes 3145732
  (21 other events, 22.9 us)
Sparse Core Ops, SparseCore 0:
  10.2 199.6 all-gather.2
where the time goes:
time: 873 us; the launch traced here: 871 us
  waiting for transfers between devices  443 us (51%)
  starting transfers between devices  143 us (16%)
  other arithmetic  111 us (13%)
  matrix products  84.4 us (10%)
  local copies, waits for them, and re-layouts  74.1 us (8%)
  between operations  14.3 us (2%)
    ppermute x16, waiting for transfers between devices, shifted(): return lax.ppermute(block, axis, route)  235 us
    all_gather x1, waiting for transfers between devices, shards(): weight = lax.all_gather(base_weight[0], 'dp', axis=0, tiled=True)  194 us
    ppermute x16, starting transfers between devices, shifted(): return lax.ppermute(block, axis, route)  138 us
    select_n x26, other arithmetic, place(): jnp.where(active, lax.dynamic_update_index_in_dim(table, value, index, 0)...  62.3 us
    dot_general x2, matrix products, forward_full(): jnp.dot(normed, weight, preferred_element_type=jnp.float32)  33 us
    add x8, other arithmetic, backward_tick(): acc_up = acc_up + weights * seq_up[None]  32.8 us
    dot_general x2, matrix products, backward_core(): dnorm = jnp.dot(grad_out, weight.T, preferred_element_type=jnp.float32)  32 us
  transfers between devices with their start and end apart: 18, of which 10 were waited for; matrix products, arithmetic and copies ran while one was open for 11% of the time, Pallas kernels for 0%

commit v1 on v0

--- a/solution.py
+++ b/solution.py
@@ -85,7 +85,9 @@
     segments = lax.axis_size("segment")
     segment = lax.axis_index("segment")
     member = lax.axis_index("dp")
-    weight = lax.all_gather(base_weight[0], "dp", axis=0, tiled=True)
+    weight = jnp.concatenate(
+        lax.all_to_all(jnp.stack([base_weight[0]] * lax.axis_size("dp")), "dp", 0, 0), axis=0
+    )
     gain = norm_gain[0]
     micro = embeds.shape[0]
     rows = embeds.shape[2]

time: 873 us -> 1180 us (1.35)
  waiting for transfers between devices: 443 us -> 742 us
  between operations: 14.3 us -> 0.92 us
  local copies, waits for them, and re-layouts: 74.1 us -> 86.5 us
    all_to_all x0 -> x1, waiting for transfers between devices: none -> 493 us  [shards(): lax.all_to_all(jnp.stack([base_weight[0]] * lax.axis_size('dp')), 'dp', 0...]
    all_gather x1 -> x0, waiting for transfers between devices: 194 us -> none  [shards(): weight = lax.all_gather(base_weight[0], 'dp', axis=0, tiled=True)]
    another operation x16 -> x17, local copies, waits for them, and re-layouts: 0.3 us -> 12.5 us  [the longest x1 12.2 us: shards(): jnp.stack([base_weight[0]] * lax.axis_size('dp'))]
  transfers between devices with their start and end apart: 18 -> 18, of which waited for: 10 -> 10; matrix products, arithmetic and copies ran while one was open for 11% -> 8% of each run, Pallas kernels for 0% -> 0%
where the time goes in v1:
time: 1180 us
  waiting for transfers between devices  742 us (63%)
  starting transfers between devices  151 us (13%)
  other arithmetic  111 us (9%)
  local copies, waits for them, and re-layouts  86.5 us (7%)
  matrix products  84.2 us (7%)
    all_to_all x1, waiting for transfers between devices, shards(): lax.all_to_all(jnp.stack([base_weight[0]] * lax.axis_size('dp')), 'dp', 0...  493 us
    ppermute x16, waiting for transfers between devices, shifted(): return lax.ppermute(block, axis, route)  235 us
    ppermute x16, starting transfers between devices, shifted(): return lax.ppermute(block, axis, route)  138 us
    select_n x26, other arithmetic, place(): jnp.where(active, lax.dynamic_update_index_in_dim(table, value, index, 0)...  62.2 us
    dot_general x2, matrix products, forward_full(): jnp.dot(normed, weight, preferred_element_type=jnp.float32)  32.9 us
    add x8, other arithmetic, backward_tick(): acc_up = acc_up + weights * seq_up[None]  32.8 us
    dot_general x2, matrix products, backward_core(): dnorm = jnp.dot(grad_out, weight.T, preferred_element_type=jnp.float32)  32 us
  transfers between devices with their start and end apart: 18, of which 10 were waited for; matrix products, arithmetic and copies ran while one was open for 8% of the time, Pallas kernels for 0%

profile of v1, /device:TPU:0, one launch (start us, length us, event | category | flops | bytes accessed | tf_op | source)
XLA Modules:
  0.0 1175.2 jit_solution(14291795063509352815)
XLA Ops:
  0.6 12.2 %stack.3 = bf16[16,256,4096]{2,1,0:T(8,128)(2,1)} broadcast(bf16[256,4096]{1,0:T(8,128)(2,1)} %bitcast.198), dimensions={1,2} | broadcast | bytes 35651584 | tf_op jit(solution)/shard_map/stack | solution.py:89
  12.9 8.3 all-to-all-start
  26.6 3.1 bitcast_multiply_fusion
  29.7 493.2 %all-to-all-done = bf16[16,256,4096]{2,1,0:T(8,128)(2,1)} async-done(((bf16[16,256,4096]{2,1,0:T(8,128)(2,1)}), bf16[16,256,4096]{2,1,0:T(8,128)(2,1)}, u32[]{:S(2)}, u32[]{:S(2)}) %all-to-all-start) | async-done | bytes 33554464 | tf_op jit(solution)/shard_map/all_to_all | solution.py:89
  525.9 230.5 %while.40 = (s32[]{:T(128)}, bf16[128,4096]{1,0:T(8,128)(2,1)}, bf16[2,128,4096]{2,1,0:T(8,128)(2,1)S(1)}, bf16[2,128,4096]{2,1,0:T(8,128)(2,1)}, s32[]{:T(128)}...) while((s32[]{:T(128)}, bf16[128,4096]{1,0:T(8,128)(2,1)}, ...), condition=%wide.region_5.6_spmd, body=%wide.region_1.5_spmd.sunk | while | flops 4321182720 | bytes 60985708 | solution.py:151
  527.7 23.1 %conditional.9 = (bf16[128,4096]{1,0:T(8,128)(2,1)}, bf16[1,128,4096]{2,1,0:T(8,128)(2,1)}) conditional(s32[]{:T(128)} %convert_element_type.345, () %tuple.153, (bf16[128,4096]{1,0:T(8,128)(2,1)S(1)}, f32[1,4096]{1,0:T(1,128)S(1)}, bf16[4096,4096]{1,0:T(8,128)(2,1)}, s32[]{:T(128)}, bf16[2,8,4096]{2,1,0:T(8,128)(2,1)S(1)}, ...), branch_computations={%region_2.2_spmd, %region_3.4_spmd} | conditional | flops 4319609856 | bytes 44207664 | solution.py:131
  528.0 16.4 %convolution_add_fusion.1 = f32[128,4096]{1,0:T(8,128)} fusion(bf16[4096,4096]{1,0:T(8,128)(2,1)} %get-tuple-element.684, bf16[128,4096]{1,0:T(8,128)(2,1)S(1)} %get-tuple-element.682, f32[4096]{0:T(1024)S(1)} %bitcast.186, f32[128]{0:T(128)S(1)} %add_rsqrt_fusion), kind=kOutput, calls=%fused_computation.1 | convolution fusion | flops 4298113024 | bytes 36717056 | tf_op jit(solution)/shard_map/while/body/eval_jaxpr/cond/branch_1_fun/dot_general | solution.py:45
  544.5 4.1 fusion
  552.2 2.8 select_dynamic-update-slice_fusion.4
  557.8 23.1 %conditional.9 = (bf16[128,4096]{1,0:T(8,128)(2,1)}, bf16[1,128,4096]{2,1,0:T(8,128)(2,1)}) conditional(s32[]{:T(128)} %convert_element_type.345, () %tuple.153, (bf16[128,4096]{1,0:T(8,128)(2,1)S(1)}, f32[1,4096]{1,0:T(1,128)S(1)}, bf16[4096,4096]{1,0:T(8,128)(2,1)}, s32[]{:T(128)}, bf16[2,8,4096]{2,1,0:T(8,128)(2,1)S(1)}, ...), branch_computations={%region_2.2_spmd, %region_3.4_spmd} | conditional | flops 4319609856 | bytes 44207664 | solution.py:131
  558.1 16.4 %convolution_add_fusion.1 = f32[128,4096]{1,0:T(8,128)} fusion(bf16[4096,4096]{1,0:T(8,128)(2,1)} %get-tuple-element.684, bf16[128,4096]{1,0:T(8,128)(2,1)S(1)} %get-tuple-element.682, f32[4096]{0:T(1024)S(1)} %bitcast.186, f32[128]{0:T(128)S(1)} %add_rsqrt_fusion), kind=kOutput, calls=%fused_computation.1 | convolution fusion | flops 4298113024 | bytes 36717056 | tf_op jit(solution)/shard_map/while/body/eval_jaxpr/cond/branch_1_fun/dot_general | solution.py:45
  574.6 4.1 fusion
  583.2 2.8 select_dynamic-update-slice_fusion.4
  591.1 32.3 %collective-permute-start = (bf16[128,4096]{1,0:T(8,128)(2,1)}, bf16[128,4096]{1,0:T(8,128)(2,1)S(1)}, u32[]{:S(2)}, u32[]{:S(2)}) collective-permute-start(bf16[128,4096]{1,0:T(8,128)(2,1)} %get-tuple-element.1159), channel_id=1, source_target_pairs={{0,16},{16,32},{32,48},{48,64},{64,80},{80,96},{96,112},{1,17},{17... | collective-permute-start | bytes 3145736 | tf_op jit(solution)/shard_map/while/body/eval_jaxpr/ppermute | solution.py:12
  623.5 2.5 select_dynamic-update-slice_fusion.4
  631.1 14.1 %collective-permute-start = (bf16[128,4096]{1,0:T(8,128)(2,1)}, bf16[128,4096]{1,0:T(8,128)(2,1)S(1)}, u32[]{:S(2)}, u32[]{:S(2)}) collective-permute-start(bf16[128,4096]{1,0:T(8,128)(2,1)} %get-tuple-element.1159), channel_id=1, source_target_pairs={{0,16},{16,32},{32,48},{48,64},{64,80},{80,96},{96,112},{1,17},{17... | collective-permute-start | bytes 3145736 | tf_op jit(solution)/shard_map/while/body/eval_jaxpr/ppermute | solution.py:12
  645.2 2.5 select_dynamic-update-slice_fusion.4
  652.7 35.0 %collective-permute-start = (bf16[128,4096]{1,0:T(8,128)(2,1)}, bf16[128,4096]{1,0:T(8,128)(2,1)S(1)}, u32[]{:S(2)}, u32[]{:S(2)}) collective-permute-start(bf16[128,4096]{1,0:T(8,128)(2,1)} %get-tuple-element.1159), channel_id=1, source_target_pairs={{0,16},{16,32},{32,48},{48,64},{64,80},{80,96},{96,112},{1,17},{17... | collective-permute-start | bytes 3145736 | tf_op jit(solution)/shard_map/while/body/eval_jaxpr/ppermute | solution.py:12
  695.3 14.1 %collective-permute-start = (bf16[128,4096]{1,0:T(8,128)(2,1)}, bf16[128,4096]{1,0:T(8,128)(2,1)S(1)}, u32[]{:S(2)}, u32[]{:S(2)}) collective-permute-start(bf16[128,4096]{1,0:T(8,128)(2,1)} %get-tuple-element.1159), channel_id=1, source_target_pairs={{0,16},{16,32},{32,48},{48,64},{64,80},{80,96},{96,112},{1,17},{17... | collective-permute-start | bytes 3145736 | tf_op jit(solution)/shard_map/while/body/eval_jaxpr/ppermute | solution.py:12
  717.0 14.1 %collective-permute-start = (bf16[128,4096]{1,0:T(8,128)(2,1)}, bf16[128,4096]{1,0:T(8,128)(2,1)S(1)}, u32[]{:S(2)}, u32[]{:S(2)}) collective-permute-start(bf16[128,4096]{1,0:T(8,128)(2,1)} %get-tuple-element.1159), channel_id=1, source_target_pairs={{0,16},{16,32},{32,48},{48,64},{64,80},{80,96},{96,112},{1,17},{17... | collective-permute-start | bytes 3145736 | tf_op jit(solution)/shard_map/while/body/eval_jaxpr/ppermute | solution.py:12
  738.7 14.1 %collective-permute-start = (bf16[128,4096]{1,0:T(8,128)(2,1)}, bf16[128,4096]{1,0:T(8,128)(2,1)S(1)}, u32[]{:S(2)}, u32[]{:S(2)}) collective-permute-start(bf16[128,4096]{1,0:T(8,128)(2,1)} %get-tuple-element.1159), channel_id=1, source_target_pairs={{0,16},{16,32},{32,48},{48,64},{64,80},{80,96},{96,112},{1,17},{17... | collective-permute-start | bytes 3145736 | tf_op jit(solution)/shard_map/while/body/eval_jaxpr/ppermute | solution.py:12
  756.4 2.8 fusion.140
  761.8 354.4 %while.41 = (s32[]{:T(128)}, bf16[128,4096]{1,0:T(8,128)(2,1)}, bf16[2,128,4096]{2,1,0:T(8,128)(2,1)}, f32[16,8,4096]{2,1,0:T(8,128)}, f32[16,8,4096]{2,1,0:T(8,...) while((s32[]{:T(128)}, bf16[128,4096]{1,0:T(8,128)(2,1)}, ...), condition=%wide.region_14.15_spmd.clone, body=%wide.region_9.14_spmd.clone.sunk | while | flops 4354214400 | bytes 94118616 | solution.py:191
  768.7 2.7 select_add_fusion.3
  771.4 25.1 %collective-permute-done.1 = bf16[128,4096]{1,0:T(8,128)(2,1)S(1)} collective-permute-done((bf16[128,4096]{1,0:T(8,128)(2,1)}, bf16[128,4096]{1,0:T(8,128)(2,1)S(1)}, u32[]{:S(2)}, u32[]{:S(2)}) %collective-permute-start.1) | collective-permute-done | bytes 1048608 | tf_op jit(solution)/shard_map/while/body/eval_jaxpr/ppermute | solution.py:12
  804.3 4.3 select_add_fusion.3
  808.6 8.1 collective-permute-done.1
  824.5 4.3 select_add_fusion.3
  828.8 7.4 collective-permute-done.1
  844.0 4.3 select_add_fusion.3
  848.3 7.9 collective-permute-done.1
  864.0 4.3 select_add_fusion.3
  868.3 23.3 %collective-permute-done.1 = bf16[128,4096]{1,0:T(8,128)(2,1)S(1)} collective-permute-done((bf16[128,4096]{1,0:T(8,128)(2,1)}, bf16[128,4096]{1,0:T(8,128)(2,1)S(1)}, u32[]{:S(2)}, u32[]{:S(2)}) %collective-permute-start.1) | collective-permute-done | bytes 1048608 | tf_op jit(solution)/shard_map/while/body/eval_jaxpr/ppermute | solution.py:12
  899.5 4.3 select_add_fusion.3
  903.8 8.1 collective-permute-done.1
  919.6 4.3 select_add_fusion.3
  923.9 148.1 %collective-permute-done.1 = bf16[128,4096]{1,0:T(8,128)(2,1)S(1)} collective-permute-done((bf16[128,4096]{1,0:T(8,128)(2,1)}, bf16[128,4096]{1,0:T(8,128)(2,1)S(1)}, u32[]{:S(2)}, u32[]{:S(2)}) %collective-permute-start.1) | collective-permute-done | bytes 1048608 | tf_op jit(solution)/shard_map/while/body/eval_jaxpr/ppermute | solution.py:12
  1073.1 25.8 %conditional.10 = (bf16[128,4096]{1,0:T(8,128)(2,1)}, f32[8,4096]{1,0:T(8,128)S(1)}, f32[8,4096]{1,0:T(8,128)S(1)}, bf16[1,128,4096]{2,1,0:T(8,128)(2,1)}) conditional(s32[]{:T(128)} %convert_element_type.346, () %tuple.157, (pred[]{:T(512)}, bf16[2,128,4096]{2,1,0:T(8,128)(2,1)}, s32[]{:T(128)}, bf16[128,4096]{1,0:T(8,128)(2,1)}, ...), branch_computations={%region_10.10_spmd, %region_11.13_spmd} | conditional | flops 4350544384 | bytes 57155172 | solution.py:170
  1076.0 16.0 %fusion.153 = f32[128,4096]{1,0:T(8,128)S(1)} fusion(bf16[128,4096]{1,0:T(8,128)(2,1)S(1)} %bitcast_select_fusion.2, bf16[4096,4096]{1,0:T(8,128)(2,1)} %get-tuple-element.714), kind=kOutput, calls=%fused_computation.169 | convolution fusion | flops 4294967296 | bytes 36700160 | tf_op jit(solution)/shard_map/while/body/eval_jaxpr/cond/branch_1_fun/dot_general | solution.py:52
  1101.1 2.8 select_dynamic-update-slice_fusion.5
  1103.8 4.3 select_add_fusion.3
  1108.1 7.1 collective-permute-done.1
  1116.2 23.6 %conditional.5 = (f32[8,4096]{1,0:T(8,128)}, f32[8,4096]{1,0:T(8,128)}, bf16[1,128,4096]{2,1,0:T(8,128)(2,1)}) conditional(s32[]{:T(128)} %convert_element_type.171, () %tuple.98, (pred[]{:T(512)}, bf16[2,128,4096]{2,1,0:T(8,128)(2,1)}, s32[]{:T(128)}, bf16[128,4096]{1,0:T(8,128)(2,1)}, bf16[2,8,4096]{2,0,1:T(2,128)(2,1)}, ...), branch_computations={%region_15.16_spmd, %region_16.19_spmd} | conditional | flops 4350544384 | bytes 56620128 | solution.py:170
  1118.4 16.0 %fusion.154 = f32[128,4096]{1,0:T(8,128)S(1)} fusion(bf16[128,4096]{1,0:T(8,128)(2,1)S(1)} %bitcast_select_fusion.3, bf16[4096,4096]{1,0:T(8,128)(2,1)} %get-tuple-element.744), kind=kOutput, calls=%fused_computation.170 | convolution fusion | flops 4294967296 | bytes 36700160 | tf_op jit(solution)/shard_map/cond/branch_1_fun/dot_general | solution.py:52
  1139.8 2.8 add_convert_fusion.1
  1145.6 4.6 all-to-all-start.1
  1155.3 4.0 bitcast_dynamic-update-slice_fusion
  1159.3 13.3 %all-to-all-done.1 = bf16[16,32,8,256]{3,2,1,0:T(8,128)(2,1)} async-done(((bf16[16,32,8,256]{3,2,1,0:T(8,128)(2,1)}), bf16[16,32,8,256]{3,2,1,0:T(8,128)(2,1)}, u32[]{:S(2)}, u32[]{:S(2)}) %all-to-all-start.1) | async-done | bytes 2097184 | tf_op jit(solution)/shard_map/all_to_all | solution.py:22
  (250 shorter events, 180.9 us)
Async XLA Ops:
  0.6 21.1 %copy-start = (bf16[1,16,8,4096]{3,2,1,0:T(8,128)(2,1)S(1)}, bf16[1,16,8,4096]{3,2,1,0:T(8,128)(2,1)}, u32[]{:S(2)}) copy-start(bf16[1,16,8,4096]{3,2,1,0:T(8,128)(2,1)} %param.24) | copy-start | bytes 3145732
  12.9 8.4 copy-start.22
  12.9 8.6 copy-start.18
  12.9 510.1 %all-to-all-start = ((bf16[16,256,4096]{2,1,0:T(8,128)(2,1)}), bf16[16,256,4096]{2,1,0:T(8,128)(2,1)}, u32[]{:S(2)}, u32[]{:S(2)}) async-start(bf16[16,256,4096]{2,1,0:T(8,128)(2,1)} %stack.3), calls=%async_computation | async-start | bytes 67108864 | tf_op jit(solution)/shard_map/all_to_all | solution.py:89
  21.2 4.5 copy-start.23
  21.7 8.0 copy-start.21
  23.3 6.4 copy-start.10
  25.0 4.7 copy-start.13
  523.2 2.7 copy-start.9
  550.9 4.1 collective-permute-start
  581.0 5.1 collective-permute-start
  591.1 34.9 %collective-permute-start = (bf16[128,4096]{1,0:T(8,128)(2,1)}, bf16[128,4096]{1,0:T(8,128)(2,1)S(1)}, u32[]{:S(2)}, u32[]{:S(2)}) collective-permute-start(bf16[128,4096]{1,0:T(8,128)(2,1)} %get-tuple-element.1159), channel_id=1, source_target_pairs={{0,16},{16,32},{32,48},{48,64},{64,80},{80,96},{96,112},{1,17},{17... | collective-permute-start | bytes 3145736 | tf_op jit(solution)/shard_map/while/body/eval_jaxpr/ppermute | solution.py:12
  631.1 16.6 %collective-permute-start = (bf16[128,4096]{1,0:T(8,128)(2,1)}, bf16[128,4096]{1,0:T(8,128)(2,1)S(1)}, u32[]{:S(2)}, u32[]{:S(2)}) collective-permute-start(bf16[128,4096]{1,0:T(8,128)(2,1)} %get-tuple-element.1159), channel_id=1, source_target_pairs={{0,16},{16,32},{32,48},{48,64},{64,80},{80,96},{96,112},{1,17},{17... | collective-permute-start | bytes 3145736 | tf_op jit(solution)/shard_map/while/body/eval_jaxpr/ppermute | solution.py:12
  652.7 37.5 %collective-permute-start = (bf16[128,4096]{1,0:T(8,128)(2,1)}, bf16[128,4096]{1,0:T(8,128)(2,1)S(1)}, u32[]{:S(2)}, u32[]{:S(2)}) collective-permute-start(bf16[128,4096]{1,0:T(8,128)(2,1)} %get-tuple-element.1159), channel_id=1, source_target_pairs={{0,16},{16,32},{32,48},{48,64},{64,80},{80,96},{96,112},{1,17},{17... | collective-permute-start | bytes 3145736 | tf_op jit(solution)/shard_map/while/body/eval_jaxpr/ppermute | solution.py:12
  695.3 16.6 %collective-permute-start = (bf16[128,4096]{1,0:T(8,128)(2,1)}, bf16[128,4096]{1,0:T(8,128)(2,1)S(1)}, u32[]{:S(2)}, u32[]{:S(2)}) collective-permute-start(bf16[128,4096]{1,0:T(8,128)(2,1)} %get-tuple-element.1159), channel_id=1, source_target_pairs={{0,16},{16,32},{32,48},{48,64},{64,80},{80,96},{96,112},{1,17},{17... | collective-permute-start | bytes 3145736 | tf_op jit(solution)/shard_map/while/body/eval_jaxpr/ppermute | solution.py:12
  717.0 16.6 %collective-permute-start = (bf16[128,4096]{1,0:T(8,128)(2,1)}, bf16[128,4096]{1,0:T(8,128)(2,1)S(1)}, u32[]{:S(2)}, u32[]{:S(2)}) collective-permute-start(bf16[128,4096]{1,0:T(8,128)(2,1)} %get-tuple-element.1159), channel_id=1, source_target_pairs={{0,16},{16,32},{32,48},{48,64},{64,80},{80,96},{96,112},{1,17},{17... | collective-permute-start | bytes 3145736 | tf_op jit(solution)/shard_map/while/body/eval_jaxpr/ppermute | solution.py:12
  738.7 16.6 %collective-permute-start = (bf16[128,4096]{1,0:T(8,128)(2,1)}, bf16[128,4096]{1,0:T(8,128)(2,1)S(1)}, u32[]{:S(2)}, u32[]{:S(2)}) collective-permute-start(bf16[128,4096]{1,0:T(8,128)(2,1)} %get-tuple-element.1159), channel_id=1, source_target_pairs={{0,16},{16,32},{32,48},{48,64},{64,80},{80,96},{96,112},{1,17},{17... | collective-permute-start | bytes 3145736 | tf_op jit(solution)/shard_map/while/body/eval_jaxpr/ppermute | solution.py:12
  764.0 32.4 %collective-permute-start.1 = (bf16[128,4096]{1,0:T(8,128)(2,1)}, bf16[128,4096]{1,0:T(8,128)(2,1)S(1)}, u32[]{:S(2)}, u32[]{:S(2)}) collective-permute-start(bf16[128,4096]{1,0:T(8,128)(2,1)} %get-tuple-element.1176), channel_id=1, source_target_pairs={{16,0},{32,16},{48,32},{64,48},{80,64},{96,80},{112,96},{17,1},{33... | collective-permute-start | bytes 3145736 | tf_op jit(solution)/shard_map/while/body/eval_jaxpr/ppermute | solution.py:12
  765.3 3.3 copy-start.2
  771.4 25.1 %copy-start.3 = (f32[16,8,4096]{2,1,0:T(8,128)}, f32[16,8,4096]{2,1,0:T(8,128)S(1)}, u32[]{:S(2)}) copy-start(f32[16,8,4096]{2,1,0:T(8,128)S(1)} %get-tuple-element.1273) | copy-start | bytes 6291460 | tf_op jit(solution)/shard_map/while
  799.7 17.0 %collective-permute-start.1 = (bf16[128,4096]{1,0:T(8,128)(2,1)}, bf16[128,4096]{1,0:T(8,128)(2,1)S(1)}, u32[]{:S(2)}, u32[]{:S(2)}) collective-permute-start(bf16[128,4096]{1,0:T(8,128)(2,1)} %get-tuple-element.1176), channel_id=1, source_target_pairs={{16,0},{32,16},{48,32},{64,48},{80,64},{96,80},{112,96},{17,1},{33... | collective-permute-start | bytes 3145736 | tf_op jit(solution)/shard_map/while/body/eval_jaxpr/ppermute | solution.py:12
  801.0 3.3 copy-start.2
  808.6 8.1 copy-start.3
  819.9 16.3 %collective-permute-start.1 = (bf16[128,4096]{1,0:T(8,128)(2,1)}, bf16[128,4096]{1,0:T(8,128)(2,1)S(1)}, u32[]{:S(2)}, u32[]{:S(2)}) collective-permute-start(bf16[128,4096]{1,0:T(8,128)(2,1)} %get-tuple-element.1176), channel_id=1, source_target_pairs={{16,0},{32,16},{48,32},{64,48},{80,64},{96,80},{112,96},{17,1},{33... | collective-permute-start | bytes 3145736 | tf_op jit(solution)/shard_map/while/body/eval_jaxpr/ppermute | solution.py:12
  821.2 3.3 copy-start.2
  828.8 7.4 copy-start.3
  839.4 16.8 %collective-permute-start.1 = (bf16[128,4096]{1,0:T(8,128)(2,1)}, bf16[128,4096]{1,0:T(8,128)(2,1)S(1)}, u32[]{:S(2)}, u32[]{:S(2)}) collective-permute-start(bf16[128,4096]{1,0:T(8,128)(2,1)} %get-tuple-element.1176), channel_id=1, source_target_pairs={{16,0},{32,16},{48,32},{64,48},{80,64},{96,80},{112,96},{17,1},{33... | collective-permute-start | bytes 3145736 | tf_op jit(solution)/shard_map/while/body/eval_jaxpr/ppermute | solution.py:12
  840.7 3.3 copy-start.2
  848.3 7.9 copy-start.3
  859.4 32.2 %collective-permute-start.1 = (bf16[128,4096]{1,0:T(8,128)(2,1)}, bf16[128,4096]{1,0:T(8,128)(2,1)S(1)}, u32[]{:S(2)}, u32[]{:S(2)}) collective-permute-start(bf16[128,4096]{1,0:T(8,128)(2,1)} %get-tuple-element.1176), channel_id=1, source_target_pairs={{16,0},{32,16},{48,32},{64,48},{80,64},{96,80},{112,96},{17,1},{33... | collective-permute-start | bytes 3145736 | tf_op jit(solution)/shard_map/while/body/eval_jaxpr/ppermute | solution.py:12
  860.7 3.3 copy-start.2
  868.3 23.3 %copy-start.3 = (f32[16,8,4096]{2,1,0:T(8,128)}, f32[16,8,4096]{2,1,0:T(8,128)S(1)}, u32[]{:S(2)}) copy-start(f32[16,8,4096]{2,1,0:T(8,128)S(1)} %get-tuple-element.1273) | copy-start | bytes 6291460 | tf_op jit(solution)/shard_map/while
  894.8 17.0 %collective-permute-start.1 = (bf16[128,4096]{1,0:T(8,128)(2,1)}, bf16[128,4096]{1,0:T(8,128)(2,1)S(1)}, u32[]{:S(2)}, u32[]{:S(2)}) collective-permute-start(bf16[128,4096]{1,0:T(8,128)(2,1)} %get-tuple-element.1176), channel_id=1, source_target_pairs={{16,0},{32,16},{48,32},{64,48},{80,64},{96,80},{112,96},{17,1},{33... | collective-permute-start | bytes 3145736 | tf_op jit(solution)/shard_map/while/body/eval_jaxpr/ppermute | solution.py:12
  896.1 3.3 copy-start.2
  903.7 8.1 copy-start.3
  915.0 157.1 %collective-permute-start.1 = (bf16[128,4096]{1,0:T(8,128)(2,1)}, bf16[128,4096]{1,0:T(8,128)(2,1)S(1)}, u32[]{:S(2)}, u32[]{:S(2)}) collective-permute-start(bf16[128,4096]{1,0:T(8,128)(2,1)} %get-tuple-element.1176), channel_id=1, source_target_pairs={{16,0},{32,16},{48,32},{64,48},{80,64},{96,80},{112,96},{17,1},{33... | collective-permute-start | bytes 3145736 | tf_op jit(solution)/shard_map/while/body/eval_jaxpr/ppermute | solution.py:12
  916.3 3.3 copy-start.2
  923.9 148.1 %copy-start.3 = (f32[16,8,4096]{2,1,0:T(8,128)}, f32[16,8,4096]{2,1,0:T(8,128)S(1)}, u32[]{:S(2)}) copy-start(f32[16,8,4096]{2,1,0:T(8,128)S(1)} %get-tuple-element.1273) | copy-start | bytes 6291460 | tf_op jit(solution)/shard_map/while
  1076.0 16.0 %copy-start.17 = (bf16[128,8]{0,1:T(8,128)(2,1)}, bf16[128,8]{0,1:T(8,128)(2,1)S(1)}, u32[]{:S(2)}) copy-start(bf16[128,8]{0,1:T(8,128)(2,1)S(1)} %convolution_convert_fusion.1) | copy-start | bytes 6148 | tf_op jit(solution)/shard_map/while/body/eval_jaxpr/cond
  1092.8 4.1 copy-start.19
  1098.9 16.3 %collective-permute-start.1 = (bf16[128,4096]{1,0:T(8,128)(2,1)}, bf16[128,4096]{1,0:T(8,128)(2,1)S(1)}, u32[]{:S(2)}, u32[]{:S(2)}) collective-permute-start(bf16[128,4096]{1,0:T(8,128)(2,1)} %get-tuple-element.1176), channel_id=1, source_target_pairs={{16,0},{32,16},{48,32},{64,48},{80,64},{96,80},{112,96},{17,1},{33... | collective-permute-start | bytes 3145736 | tf_op jit(solution)/shard_map/while/body/eval_jaxpr/ppermute | solution.py:12
  1100.2 3.6 copy-start.2
  1108.1 7.1 copy-start.3
  1118.4 16.0 %copy-start.12 = (bf16[2,8,4096]{2,0,1:T(2,128)(2,1)S(1)}, bf16[2,8,4096]{2,0,1:T(2,128)(2,1)}, u32[]{:S(2)}) copy-start(bf16[2,8,4096]{2,0,1:T(2,128)(2,1)} %get-tuple-element.936) | copy-start | bytes 393220 | tf_op jit(solution)/shard_map/cond
  1145.6 4.6 copy-start.4
  1145.6 27.0 %all-to-all-start.1 = ((bf16[16,32,8,256]{3,2,1,0:T(8,128)(2,1)}), bf16[16,32,8,256]{3,2,1,0:T(8,128)(2,1)}, u32[]{:S(2)}, u32[]{:S(2)}) async-start(bf16[16,32,8,256]{3,2,1,0:T(8,128)(2,1)} %copy.43), calls=%async_computation.1 | async-start | bytes 4194304 | tf_op jit(solution)/shard_map/all_to_all | solution.py:22
  1150.3 2.6 copy-start.14
  1155.3 19.9 %copy-start.1 = (bf16[1,16,8,4096]{3,2,1,0:T(8,128)(2,1)S(1)}, bf16[1,16,8,4096]{3,2,1,0:T(8,128)(2,1)}, u32[]{:S(2)}) copy-start(bf16[1,16,8,4096]{3,2,1,0:T(8,128)(2,1)} %param.24) | copy-start | bytes 3145732
  (21 other events, 27.6 us)
